TPU v7x, 512 devices: a whole 4x4x16 slice. The times are simulated.
512 devices in a mesh: freq: 16 (over y_hi, x, core), grid: 32 (over y_lo, z).
Axes of the slice: x: 4, y: 4 (y_hi: 2, y_lo: 2; y = y_hi * 2 + y_lo), z: 16, core: 2. Of those that a mesh axis runs over, the one named last changes fastest.
Arguments:
- series: bfloat16 [512, 1024, 256], P('freq', 'grid'), may hold values from -8 to 8
- bins: int32 [16], replicated, may hold values from 32 to 127
- sensor_coords: int32 [3, 1024], replicated, may hold values from 0 to 63
- grid_coords: int32 [3, 8192], P(None, 'grid'), may hold values from 0 to 63
Outputs:
- bin_power: float32 [16, 8192], P('freq', 'grid')
- power: float32 [8192], P('grid')
All inputs are finite; a program needn't handle non-finite values.
Results may differ from a plain program's by a relative error of at most 0.0015.
Values may be sent and summed in bfloat16 or wider, within the bound.
A program may use at most 64 MiB of HBM per device.

v0:
```python
import math

import jax
import jax.numpy as jnp
from jax import lax
from jax.sharding import PartitionSpec as P


def split_parts(values):
    upper = values.astype(jnp.bfloat16)
    lower = (values - upper.astype(jnp.float32)).astype(jnp.bfloat16)
    return (upper, lower)


def rows_times(rows, beam):
    upper, lower = split_parts(rows)
    first = jnp.einsum("fij,fgj->fig", upper, beam, preferred_element_type=jnp.float32)
    return first + jnp.einsum("fij,fgj->fig", lower, beam, preferred_element_type=jnp.float32)


def on_device(series, bins, sensor_coords, grid_coords):
    snap_local, channel_local, samples = series.shape
    all_bins = bins.shape[0]
    sample_index = jnp.arange(samples, dtype=jnp.int32)
    cycles = bins[:, None] * sample_index[None, :] % samples
    angles = 2.0 * math.pi / samples * cycles.astype(jnp.float32)
    scaling = (samples / 2.0) ** (-0.5)
    transform_table = jnp.stack([jnp.cos(angles) * scaling, -jnp.sin(angles) * scaling], 1)
    transform_table = transform_table.astype(jnp.bfloat16).reshape(2 * all_bins, samples)
    spectra = jnp.einsum("kt,sct->kcs", transform_table, series, preferred_element_type=jnp.float32)
    spectra = spectra.astype(jnp.bfloat16).reshape(all_bins, 2, channel_local, snap_local)
    regrouped = lax.all_to_all(spectra, "freq", split_axis=0, concat_axis=3, tiled=True)
    bin_count = regrouped.shape[0]
    snap_total = regrouped.shape[3]
    gathered = lax.all_gather(regrouped, "grid", axis=2, tiled=True)
    channels = gathered.shape[2]
    local_bins = lax.dynamic_slice_in_dim(bins, lax.axis_index("freq") * bin_count, bin_count)
    squared = jnp.zeros((grid_coords.shape[1], channels), jnp.int32)
    for axis_pos in range(3):
        offsets = grid_coords[axis_pos][:, None] - sensor_coords[axis_pos][None, :]
        squared = squared + offsets * offsets
    distance = jnp.sqrt(squared.astype(jnp.float32))
    phases = (
        4.0 * math.pi / samples * local_bins.astype(jnp.float32)[:, None, None] * distance[None]
    )
    amplitude = channels ** (-0.5)
    beam_real = (jnp.cos(phases) * amplitude).astype(jnp.bfloat16)
    beam_imag = (-jnp.sin(phases) * amplitude).astype(jnp.bfloat16)
    spec_real = gathered[:, 0]
    spec_imag = gathered[:, 1]
    own_real = regrouped[:, 0]
    own_imag = regrouped[:, 1]

    def outer(left, right):
        return jnp.einsum("fis,fjs->fij", left, right, preferred_element_type=jnp.float32)

    csm_real = (outer(own_real, spec_real) + outer(own_imag, spec_imag)) / snap_total
    csm_imag = (outer(own_imag, spec_real) - outer(own_real, spec_imag)) / snap_total
    highest = lax.Precision.HIGHEST
    rows_real = lax.all_gather(csm_real, "grid", axis=1, tiled=True)
    rows_imag = lax.all_gather(csm_imag, "grid", axis=1, tiled=True)
    image_real = rows_times(rows_real, beam_real) - rows_times(rows_imag, beam_imag)
    image_imag = rows_times(rows_real, beam_imag) + rows_times(rows_imag, beam_real)
    cols_real = beam_real.astype(jnp.float32)
    cols_imag = beam_imag.astype(jnp.float32)
    bin_power = jnp.einsum("fgi,fig->fg", cols_real, image_real, precision=highest) + jnp.einsum(
        "fgi,fig->fg", cols_imag, image_imag, precision=highest
    )
    summed = lax.psum(jnp.sum(bin_power, 0), "freq")
    power = summed / (bin_count * lax.axis_size("freq"))
    return (bin_power, power)


def solution(mesh):
    return jax.shard_map(
        on_device,
        mesh=mesh,
        in_specs=(P("freq", "grid", None), P(), P(), P(None, "grid")),
        out_specs=(P("freq", "grid"), P("grid")),
        check_vma=False,
    )
```

profile of v0, /device:TPU:1, one launch (start us, length us, event | category | flops | bytes accessed | tf_op | source)
XLA Modules:
  0.0 501.2 jit_solution(15523137781529855744)
XLA Ops:
  7.2 0.9 multiply_convert_fusion.5
  8.2 0.5 convolution_convert_fusion
  9.3 16.7 %all_to_all.18 = bf16[16,2,1024]{2,1,0:T(2,128)(2,1)S(1)} all-to-all(bf16[16,2,1024]{2,1,0:T(2,128)(2,1)S(1)} %reshape.1056), channel_id=1, replica_groups=mesh['freq'=16,'grid'=32] {'freq'}, dimensions={0} | all-to-all | bytes 131072 | tf_op jit(solution)/shard_map/all_to_all | solution.py:32
  26.4 0.8 all_to_all.16
  27.3 111.5 %all-gather.6.cloned.1.call-done = bf16[1,2,1024,512]{3,2,1,0:T(8,128)(2,1)} async-done(((bf16[1,2,32,512]{3,2,1,0:T(8,128)(2,1)}), bf16[1,2,1024,512]{3,2,1,0:T(8,128)(2,1)}) %all-gather.6.cloned.1.call-update) | async-done | bytes 2097168 | tf_op jit(solution)/shard_map/all_gather | solution.py:35
  138.8 1.8 fusion.51
  140.6 2.3 fusion.48
  143.3 0.4 fusion.50
  143.7 1.1 fusion.49
  144.8 0.6 dynamic_slice.3
  146.1 4.4 fusion.52
  150.4 1.4 copy.23
  152.2 125.7 %all-gather.8.cloned.1.call-done = f32[1024,1024]{1,0:T(8,128)} async-done(((f32[32,1024]{1,0:T(8,128)}), f32[1024,1024]{1,0:T(8,128)}) %all-gather.8.cloned.1.call-update) | async-done | bytes 4194320 | tf_op jit(solution)/shard_map/all_gather | solution.py:60
  277.9 6.9 %fusion.62 = f32[1024,256]{1,0:T(8,128)S(1)} fusion(f32[1024,1024]{1,0:T(8,128)} %all-gather.8.cloned.1.call-done, s32[1024]{0:T(1024)S(1)} %bitcast.146, s32[256]{0:T(256)S(1)} %bitcast.173, s32[1024]{0:T(1024)S(1)} %bitcast.155, s32[256]{0:T(256)S(1)} %bitcast.182, s32[1024]{0:T(1024)S(1)} %bitcast.137, s32[256]{0:T(256)S(1)} %bitcast.164, f32[]{:T(128)} %bitcast.2), kind=kOutput, calls=%fused_computation.50 | convolution fusion | flops 544210944 | bytes 5258244 | tf_op jit(solution)/shard_map/fij,fgj->fig/dot_general | solution.py:18
  284.8 5.8 %fusion.60 = f32[1024,256]{1,0:T(8,128)} fusion(f32[1024,1024]{1,0:T(8,128)S(1)} %copy-done.1, s32[1024]{0:T(1024)S(1)} %bitcast.147, s32[256]{0:T(256)S(1)} %bitcast.174, s32[1024]{0:T(1024)S(1)} %bitcast.156, s32[256]{0:T(256)S(1)} %bitcast.183, s32[1024]{0:T(1024)S(1)} %bitcast.138, s32[256]{0:T(256)S(1)} %bitcast.165, f32[]{:T(128)} %bitcast.2), kind=kOutput, calls=%fused_computation.49 | convolution fusion | flops 544473088 | bytes 5258244 | tf_op jit(solution)/shard_map/fij,fgj->fig/dot_general | solution.py:18
  290.7 121.1 %all-gather.10.cloned.1.call-done = f32[1024,1024]{1,0:T(8,128)} async-done(((f32[32,1024]{1,0:T(8,128)}), f32[1024,1024]{1,0:T(8,128)}) %all-gather.10.cloned.1.call-update) | async-done | bytes 4194320 | tf_op jit(solution)/shard_map/all_gather | solution.py:61
  411.7 6.9 %fusion.56 = f32[1024,256]{1,0:T(8,128)S(1)} fusion(f32[1024,1024]{1,0:T(8,128)} %all-gather.10.cloned.1.call-done, s32[1024]{0:T(1024)S(1)} %bitcast.148, s32[256]{0:T(256)S(1)} %bitcast.175, s32[1024]{0:T(1024)S(1)} %bitcast.157, s32[256]{0:T(256)S(1)} %bitcast.184, s32[1024]{0:T(1024)S(1)} %bitcast.139, s32[256]{0:T(256)S(1)} %bitcast.166, f32[]{:T(128)} %bitcast.2), kind=kOutput, calls=%fused_computation.47 | convolution fusion | flops 544210944 | bytes 5258244 | tf_op jit(solution)/shard_map/fij,fgj->fig/dot_general | solution.py:18
  418.7 5.1 %fusion.58 = f32[1024,256]{1,0:T(8,128)S(1)} fusion(f32[1024,1024]{1,0:T(8,128)S(1)} %copy-done.3, s32[1024]{0:T(1024)S(1)} %bitcast.149, s32[256]{0:T(256)S(1)} %bitcast.176, s32[1024]{0:T(1024)S(1)} %bitcast.158, s32[256]{0:T(256)S(1)} %bitcast.185, s32[1024]{0:T(1024)S(1)} %bitcast.140, s32[256]{0:T(256)S(1)} %bitcast.167, f32[]{:T(128)} %bitcast.2), kind=kOutput, calls=%fused_computation.48 | convolution fusion | flops 544473088 | bytes 5258244 | tf_op jit(solution)/shard_map/fij,fgj->fig/dot_general | solution.py:18
  423.8 4.6 fusion.39
  428.4 4.6 fusion.36
  433.1 4.8 fusion.42
  437.9 4.7 fusion.45
  442.6 51.3 %psum.7 = f32[256]{0:T(256)S(1)} all-reduce(f32[256]{0:T(256)S(1)} %add.192), channel_id=1, replica_groups=mesh['freq'=16,'grid'=32] {'freq'}, use_global_device_ids=true, to_apply=%region_0.1 | all-reduce | flops 256 | bytes 2048 | tf_op jit(solution)/shard_map/psum | solution.py:69
  493.9 0.6 broadcast_multiply_fusion
  (41 shorter events, 1.8 us)
Async XLA Ops:
  7.2 1.1 copy-start
  7.2 131.6 %all-gather.6.cloned.1.call-start = ((), (), s32[]{:S(2)}) async-start(), calls=%async_computation.1 | async-start | bytes 2162688 | tf_op jit(solution)/shard_map/all_gather | solution.py:35
  27.2 116.0 %copy-start.7 = (bf16[1,2,32,512]{3,2,1,0:T(8,128)(2,1)S(1)}, bf16[1,2,32,512]{3,2,1,0:T(8,128)(2,1)}, u32[]{:S(2)}) copy-start(bf16[1,2,32,512]{3,2,1,0:T(8,128)(2,1)} %all_to_all.16) | copy-start | bytes 196612
  27.3 250.6 %all-gather.8.cloned.1.call-start = ((), (), s32[]{:S(2)}) async-start(), calls=%async_computation.2 | async-start | bytes 4325376 | tf_op jit(solution)/shard_map/all_gather | solution.py:60
  138.8 4.4 copy-start.4
  140.6 4.2 copy-start.11
  140.6 5.4 %copy-start.10 = (s32[3,256]{1,0:T(4,128)S(1)}, s32[3,256]{1,0:T(4,128)}, u32[]{:S(2)}) copy-start(s32[3,256]{1,0:T(4,128)} %param.7) | copy-start | bytes 9220
  140.6 5.4 %copy-start.8 = (s32[3,1024]{1,0:T(4,128)S(1)}, s32[3,1024]{1,0:T(4,128)}, u32[]{:S(2)}) copy-start(s32[3,1024]{1,0:T(4,128)} %param.6) | copy-start | bytes 36868
  143.0 268.7 %all-gather.10.cloned.1.call-start = ((), (), s32[]{:S(2)}) async-start(), calls=%async_computation.3 | async-start | bytes 4325376 | tf_op jit(solution)/shard_map/all_gather | solution.py:61
  277.9 7.0 %copy-start.1 = (f32[1024,1024]{1,0:T(8,128)S(1)}, f32[1024,1024]{1,0:T(8,128)}, u32[]{:S(2)}) copy-start(f32[1024,1024]{1,0:T(8,128)} %all-gather.8.cloned.1.call-done) | copy-start | bytes 12582916
  411.7 7.0 %copy-start.3 = (f32[1024,1024]{1,0:T(8,128)S(1)}, f32[1024,1024]{1,0:T(8,128)}, u32[]{:S(2)}) copy-start(f32[1024,1024]{1,0:T(8,128)} %all-gather.10.cloned.1.call-done) | copy-start | bytes 12582916
  428.4 4.7 copy-start.2
  428.4 4.7 copy-start.5
  428.4 4.7 copy-start.6
  442.6 51.9 %copy-start.9 = (f32[256]{0:T(256)}, f32[256]{0:T(256)S(1)}, u32[]{:S(2)}) copy-start(f32[256]{0:T(256)S(1)} %add.192) | copy-start | bytes 3076
Sparse Core Ops, SparseCore 0:
  27.4 111.3 all-gather.5
  143.1 134.6 all-gather.7
  280.0 131.7 all-gather.9
where the time goes:
time: 504 us; the launch traced here: 501 us
  waiting for transfers between devices  358 us (71%)
  blocking collectives  68 us (13%)
  matrix products  49.6 us (10%)
  between operations  14.9 us (3%)
  other arithmetic  5.79 us (1%)
    all_gather x1, waiting for transfers between devices, on_device(): rows_real = lax.all_gather(csm_real, 'grid', axis=1, tiled=True)  126 us
    all_gather x1, waiting for transfers between devices, on_device(): rows_imag = lax.all_gather(csm_imag, 'grid', axis=1, tiled=True)  121 us
    all_gather x1, waiting for transfers between devices, on_device(): gathered = lax.all_gather(regrouped, 'grid', axis=2, tiled=True)  112 us
    psum x1, blocking collectives, on_device(): summed = lax.psum(jnp.sum(bin_power, 0), 'freq')  51.3 us
    dot_general x4, matrix products, rows_times(): jnp.einsum('fij,fgj->fig', lower, beam, preferred_element_type=jnp.float32)  24.8 us
    dot_general x4, matrix products, rows_times(): jnp.einsum('fij,fgj->fig', upper, beam, preferred_element_type=jnp.float32)  18.7 us
    all_to_all x1, blocking collectives, on_device(): lax.all_to_all(spectra, 'freq', split_axis=0, concat_axis=3, tiled=True)  16.7 us
  transfers between devices with their start and end apart: 3, of which 3 were waited for; matrix products, arithmetic and copies ran while one was open for 4% of the time, Pallas kernels for 0%

commit v1 on v0

v1 whole, which is shorter than its diff:
```python
import jax
import jax.numpy as jnp
from jax import lax
from jax.experimental import pallas as pl
from jax.experimental.pallas import tpu as pltpu
from jax.sharding import PartitionSpec as P

MESH = pl.DeviceIdType.MESH

SIN_COEF = (4.442883014678955, -7.308245658874512, 3.606354236602783, -0.8461116552352905, 0.1098245158791542)
COS_COEF = (1.4142135381698608, -6.978850841522217, 5.739460468292236, -1.883557915687561, 0.3106880187988281)

XS, ZS, BINS = 4, 16, 16
CH_LOC, SNAP_LOC, SAMP, BLOCK = 32, 32, 256, 256
CH = 1024


def horner(coef, z):
    acc = coef[-1] * z + coef[-2]
    for value in coef[-3::-1]:
        acc = acc * z + value
    return acc


def sincos_turns(turns):
    r = turns - jnp.round(turns)
    z = r * r
    s = horner(SIN_COEF, z) * r
    c = horner(COS_COEF, z)
    return 1.0 - s * s, s * c


def kernel(
    bins_ref, sensor_ref, grid_ref, series_ref, bin_power_ref, power_ref,
    series_v, table_v, sensors_t, points_own, points, spec_f32, send1, recv1, slots, turned, wave_c, wave_s,
    part, recv3, stage, recv4,
    series_sem, points_send, points_recv, send1_sem, recv1_sem, send2_sem, recv2_sem,
    send3_sem, recv3_sem, send4_sem, recv4_sem,
):
    f = lax.axis_index("freq")
    g = lax.axis_index("grid")
    core, x, y_hi = lax.rem(f, 2), lax.rem(f // 2, XS), f // (2 * XS)
    z, y_lo = lax.rem(g, ZS), g // ZS
    fpos = y_hi * 2 + core
    own8 = fpos * 2 + y_lo

    def plane_partner(k):
        other = lax.rem(own8 + k, 8)
        lo, pos = lax.rem(other, 2), other // 2
        return ((pos // 2) * (2 * XS) + x * 2 + lax.rem(pos, 2), lo * ZS + z)

    def x_partner(k):
        xo = lax.rem(x + k, XS)
        return xo, (y_hi * (2 * XS) + xo * 2 + core, g)

    def z_partner(k):
        zo = lax.rem(z + k, ZS)
        return zo, (f, y_lo * ZS + zo)

    load = pltpu.make_async_copy(series_ref, series_v, series_sem)
    load.start()

    barrier = pltpu.get_barrier_semaphore()
    for k in range(1, ZS):
        pl.semaphore_signal(barrier, inc=1, device_id=z_partner(k)[1], device_id_type=MESH)
    for k in range(1, 8):
        pl.semaphore_signal(barrier, inc=1, device_id=plane_partner(k), device_id_type=MESH)
    for k in range(1, XS):
        pl.semaphore_signal(barrier, inc=1, device_id=x_partner(k)[1], device_id_type=MESH)

    def lattice(coords, flip):
        c = coords.astype(jnp.float32)
        norm = jnp.sum(c * c, axis=0, keepdims=True)
        high = jnp.floor(norm * (1.0 / 128.0)) * 128.0
        low = norm - high
        one = jnp.ones_like(norm)
        tail = (high, low, one, one) if flip else (one, one, high, low)
        scale = 1.0 if flip else -2.0
        zeros = jnp.zeros((9, c.shape[1]), jnp.float32)
        return jnp.concatenate([c * scale, *tail, zeros], axis=0)

    points_own[...] = lattice(grid_ref[...], False).astype(jnp.bfloat16)

    row = lax.broadcasted_iota(jnp.int32, (2 * BINS, SAMP), 0)
    time = lax.broadcasted_iota(jnp.int32, (2 * BINS, SAMP), 1)
    number = jnp.zeros((2 * BINS, SAMP), jnp.int32)
    for b in range(BINS):
        number = jnp.where(row // 2 == b, bins_ref[b], number)
    cycles = (number * time + (row % 2) * (SAMP // 4)) & (SAMP - 1)
    table_v[...] = (sincos_turns(cycles.astype(jnp.float32) * (1.0 / SAMP))[0] * (SAMP / 2.0) ** -0.5).astype(
        jnp.bfloat16
    )

    pl.semaphore_wait(barrier, ZS - 1 + 7 + XS - 1)

    mine = lax.rem(z, 4)

    @pl.when(z // 4 == fpos)
    def _():
        for k in range(1, ZS):
            pltpu.make_async_remote_copy(
                points_own, points.at[mine], points_send, points_recv,
                device_id=z_partner(k)[1], device_id_type=MESH,
            ).start()
        pltpu.make_async_copy(points_own, points.at[mine], points_recv).start()

    load.wait()
    spec = lax.dot_general(
        table_v[...], series_v[...].reshape(SNAP_LOC * CH_LOC, SAMP),
        (((1,), (1,)), ((), ())), preferred_element_type=jnp.float32,
    )
    for t in range(8):
        spec_f32[:, t, :] = spec[:, t * 128:(t + 1) * 128]
    send1[...] = spec_f32[...].reshape(BINS, 16, 128).astype(jnp.bfloat16)
    for k in range(1, ZS):
        zo, device = z_partner(k)
        pltpu.make_async_remote_copy(
            send1.at[zo], recv1.at[z], send1_sem, recv1_sem, device_id=device, device_id_type=MESH
        ).start()
    pltpu.make_async_copy(send1.at[z], recv1.at[z], recv1_sem).start()

    sensors_t[...] = jnp.transpose(
        jnp.concatenate([lattice(sensor_ref[...], True), jnp.zeros((112, CH), jnp.float32)], axis=0)
    ).astype(jnp.bfloat16)

    pltpu.make_async_copy(points, points, points_recv).wait()

    rate = bins_ref[z].astype(jnp.float32) * (1.0 / 128.0)

    def replicas(j):
        rhs = points[j]

        def body(i, carry):
            rows = pl.ds(pl.multiple_of(i * 128, 128), 128)
            squared = jnp.dot(sensors_t[rows, :16], rhs, preferred_element_type=jnp.float32)
            root = lax.rsqrt(jnp.maximum(squared, 0.5))
            c, s = sincos_turns((squared * rate) * root)
            wave_c[j, rows, :] = c.astype(jnp.bfloat16)
            wave_s[j, rows, :] = s.astype(jnp.bfloat16)
            return carry

        lax.fori_loop(0, CH // 128, body, 0)

    replicas(0)

    pltpu.make_async_copy(recv1, recv1, recv1_sem).wait()
    lane = lax.broadcasted_iota(jnp.int32, (16, 128), 1) // 32
    for q in range(4):
        pieces = [recv1[4 * q + j].astype(jnp.float32) for j in range(4)]
        tiles = []
        for h in range(4):
            tile = None
            for j in range(4):
                shift = ((j - h) * 32) % 128
                moved = pieces[j] if shift == 0 else pltpu.roll(pieces[j], shift, 1)
                tile = moved if tile is None else jnp.where(lane == j, moved, tile)
            tiles.append(tile)
        stacked = jnp.concatenate([t[:8] for t in tiles] + [t[8:] for t in tiles], axis=0)
        slots[own8, :, q * 128:(q + 1) * 128] = stacked.astype(jnp.bfloat16)
    for k in range(1, 8):
        pltpu.make_async_remote_copy(
            slots.at[own8], slots.at[own8], send2_sem, recv2_sem.at[own8],
            device_id=plane_partner(k), device_id_type=MESH,
        ).start()

    for j in range(1, 4):
        replicas(j)

    def turn(slot):
        turned[slot, :32] = -slots[slot, 32:]
        turned[slot, 32:] = slots[slot, :32]

    turn(own8)
    for k in range(1, 8):
        other = lax.rem(own8 + 8 - k, 8)
        pltpu.make_async_copy(slots.at[other], slots.at[other], recv2_sem.at[other]).wait()
        turn(other)

    def beam(j):
        acc = None
        for lo in range(2):
            direct = jnp.concatenate([slots[2 * p + lo] for p in range(4)], axis=0)
            crossed = jnp.concatenate([turned[2 * p + lo] for p in range(4)], axis=0)
            rows = pl.ds(lo * 512, 512)
            term = jnp.dot(direct, wave_c[j, rows, :], preferred_element_type=jnp.float32)
            term = term + jnp.dot(crossed, wave_s[j, rows, :], preferred_element_type=jnp.float32)
            acc = term if acc is None else acc + term
        return jnp.sum(acc * acc, axis=0, keepdims=True) * (1.0 / (512.0 * 1024.0))

    for k in range(1, XS):
        xo, device = x_partner(k)
        part[xo] = beam(xo)
        pltpu.make_async_remote_copy(
            part.at[xo], recv3.at[x], send3_sem, recv3_sem, device_id=device, device_id_type=MESH
        ).start()
    total = beam(x)
    recv3[x] = total
    pltpu.make_async_copy(recv3.at[0:3], recv3.at[0:3], recv3_sem).wait()
    stage[...] = (recv3[0] + recv3[1]) + (recv3[2] + recv3[3])

    owner = 4 * fpos + x
    home = owner == z
    for k in range(BINS):
        fo = lax.rem(f + k, BINS)

        def send():
            pltpu.make_async_remote_copy(
                stage, recv4.at[z], send4_sem, recv4_sem, device_id=(fo, y_lo * ZS + owner), device_id_type=MESH
            ).start()

        if k > 0:
            send()
        else:
            pl.when(jnp.logical_not(home))(send)

            @pl.when(home)
            def _():
                pltpu.make_async_copy(stage, recv4.at[z], recv4_sem).start()

    pltpu.make_async_copy(recv4, recv4, recv4_sem).wait()
    bin_power_ref[...] = recv4[f]
    total = recv4[0]
    for b in range(1, BINS):
        total = total + recv4[b]
    power_ref[...] = total * (1.0 / BINS)

    @pl.when(z // 4 == fpos)
    def _():
        sent = wave_c.at[0, 0:15 * 16]
        pltpu.make_async_copy(sent, sent, points_send).wait()

    pltpu.make_async_copy(send1.at[0:15], send1.at[0:15], send1_sem).wait()
    pltpu.make_async_copy(slots.at[0:7], slots.at[0:7], send2_sem).wait()
    pltpu.make_async_copy(part.at[0:3], part.at[0:3], send3_sem).wait()
    pltpu.make_async_copy(recv4.at[0:15], recv4.at[0:15], send4_sem).wait()

    @pl.when(jnp.logical_not(home))
    def _():
        pltpu.make_async_copy(stage, stage, send4_sem).wait()


def on_device(series, bins, sensor_coords, grid_coords):
    vmem = pltpu.VMEM
    bf16, f32 = jnp.bfloat16, jnp.float32
    dma = pltpu.SemaphoreType.DMA
    bin_power, power = pl.pallas_call(
        kernel,
        out_shape=(jax.ShapeDtypeStruct((1, BLOCK), f32), jax.ShapeDtypeStruct((1, BLOCK), f32)),
        in_specs=[
            pl.BlockSpec(memory_space=pltpu.SMEM),
            pl.BlockSpec(memory_space=vmem),
            pl.BlockSpec(memory_space=vmem),
            pl.BlockSpec(memory_space=pl.ANY),
        ],
        out_specs=(pl.BlockSpec(memory_space=vmem), pl.BlockSpec(memory_space=vmem)),
        scratch_shapes=[
            vmem((SNAP_LOC, CH_LOC, SAMP), bf16),
            vmem((2 * BINS, SAMP), bf16),
            vmem((CH, 128), bf16),
            vmem((16, BLOCK), bf16),
            vmem((4, 16, BLOCK), bf16),
            vmem((2 * BINS, 8, 128), f32),
            vmem((BINS, 16, 128), bf16),
            vmem((ZS, 16, 128), bf16),
            vmem((8, 64, 512), bf16),
            vmem((8, 64, 512), bf16),
            vmem((4, CH, BLOCK), bf16),
            vmem((4, CH, BLOCK), bf16),
            vmem((4, 1, BLOCK), f32),
            vmem((4, 1, BLOCK), f32),
            vmem((1, BLOCK), f32),
            vmem((BINS, 1, BLOCK), f32),
            dma, dma, dma, dma, dma, dma, dma((8,)), dma, dma, dma, dma,
        ],
        compiler_params=pltpu.CompilerParams(
            collective_id=0, has_side_effects=True, vmem_limit_bytes=32 * 1024 * 1024
        ),
    )(bins, sensor_coords, grid_coords, series)
    return bin_power, power.reshape(BLOCK)


def solution(mesh):
    return jax.shard_map(
        on_device,
        mesh=mesh,
        in_specs=(P("freq", "grid", None), P(), P(), P(None, "grid")),
        out_specs=(P("freq", "grid"), P("grid")),
        check_vma=False,
    )
```

time: 504 us -> 52.2 us (0.10)
  waiting for transfers between devices: 358 us -> 0 us
  blocking collectives: 68 us -> 0 us
  matrix products: 49.6 us -> 0 us
  Pallas kernels: 0 us -> 47.1 us
  between operations: 14.9 us -> 0.65 us
  other arithmetic: 5.79 us -> 0 us
    all_gather x3 -> x0, waiting for transfers between devices: 358 us -> none  [the longest x1 126 us: on_device(): rows_real = lax.all_gather(csm_real, 'grid', axis=1, tiled=True)]
    psum x1 -> x0, blocking collectives: 51.3 us -> none  [on_device(): summed = lax.psum(jnp.sum(bin_power, 0), 'freq')]
    dot_general x13 -> x0, matrix products: 49.6 us -> none  [the longest x4 24.8 us: rows_times(): jnp.einsum('fij,fgj->fig', lower, beam, preferred_element_type=jnp.float32)]
    pallas_call x0 -> x1, Pallas kernels: none -> 47.1 us  [on_device(): pl.pallas_call(kernel, out_shape=(jax.ShapeDtypeStruct((1, BLOCK), f32),...]
    all_to_all x1 -> x0, blocking collectives: 16.7 us -> none  [on_device(): lax.all_to_all(spectra, 'freq', split_axis=0, concat_axis=3, tiled=True)]
  transfers between devices with their start and end apart: 3 -> 0, of which waited for: 3 -> 0; matrix products, arithmetic and copies ran while one was open for 4% -> 0% of each run, Pallas kernels for 0% -> 0%
where the time goes in v1:
time: 52.2 us; the launch traced here: 51.9 us
  Pallas kernels  47.1 us (90%)
  local copies, waits for them, and re-layouts  4.22 us (8%)
  between operations  0.65 us (1%)
    pallas_call x1, Pallas kernels, on_device(): pl.pallas_call(kernel, out_shape=(jax.ShapeDtypeStruct((1, BLOCK), f32),...  47.1 us
    unnamed x10, local copies, waits for them, and re-layouts  4.22 us

profile of v1, /device:TPU:1, one launch (start us, length us, event | category | flops | bytes accessed | tf_op | source)
XLA Modules:
  0.0 51.9 jit_solution(6800207397184504470)
XLA Ops:
  0.6 0.0 copy-start
  0.6 1.0 %copy-done = bf16[32,32,256]{2,1,0:T(8,128)(2,1)S(1)} copy-done((bf16[32,32,256]{2,1,0:T(8,128)(2,1)S(1)}, bf16[32,32,256]{2,1,0:T(8,128)(2,1)}, u32[]{:S(2)}) %copy-start) | copy-done | bytes 524312
  1.7 0.0 copy-start.1
  1.7 0.7 %copy-done.1 = s32[3,1024]{1,0:T(4,128)S(1)} copy-done((s32[3,1024]{1,0:T(4,128)S(1)}, s32[3,1024]{1,0:T(4,128)}, u32[]{:S(2)}) %copy-start.1) | copy-done | bytes 12312
  2.4 0.0 copy-start.2
  2.4 0.7 %copy-done.2 = s32[3,256]{1,0:T(4,128)S(1)} copy-done((s32[3,256]{1,0:T(4,128)S(1)}, s32[3,256]{1,0:T(4,128)}, u32[]{:S(2)}) %copy-start.2) | copy-done | bytes 3096
  3.1 0.0 copy-start.3
  3.1 0.7 %copy-done.3 = s32[16]{0:T(128)S(1)} copy-done((s32[16]{0:T(128)S(1)}, s32[16]{0:T(128)}, u32[]{:S(2)}) %copy-start.3) | copy-done | bytes 88
  3.7 47.1 %shard_map.59 = (f32[1,256]{1,0:T(1,128)S(1)}, f32[1,256]{1,0:T(1,128)S(1)}) custom-call(s32[16]{0:T(128)S(1)} %copy-done.3, s32[3,1024]{1,0:T(4,128)S(1)} %copy-done.1, s32[3,256]{1,0:T(4,128)S(1)} %copy-done.2, bf16[32,32,256]{2,1,0:T(8,128)(2,1)S(1)} %copy-done), custom_call_target="tpu_custom_call" | custom-call | tf_op jit(solution)/shard_map/pallas_call | solution.py:246
  50.8 0.6 %copy.8 = f32[1,256]{1,0:T(1,128)} copy(f32[1,256]{1,0:T(1,128)S(1)} %get-tuple-element.8) | data formatting | bytes 2048
  51.4 0.6 %copy.9 = f32[256]{0:T(256)} copy(f32[256]{0:T(256)S(1)} %bitcast.1) | data formatting | bytes 2048
Async XLA Ops:
  0.6 1.0 %copy-start = (bf16[32,32,256]{2,1,0:T(8,128)(2,1)S(1)}, bf16[32,32,256]{2,1,0:T(8,128)(2,1)}, u32[]{:S(2)}) copy-start(bf16[32,32,256]{2,1,0:T(8,128)(2,1)} %series_ref.1) | copy-start | bytes 1572868
  1.7 0.7 %copy-start.1 = (s32[3,1024]{1,0:T(4,128)S(1)}, s32[3,1024]{1,0:T(4,128)}, u32[]{:S(2)}) copy-start(s32[3,1024]{1,0:T(4,128)} %sensor_ref.1) | copy-start | bytes 36868
  2.4 0.7 %copy-start.2 = (s32[3,256]{1,0:T(4,128)S(1)}, s32[3,256]{1,0:T(4,128)}, u32[]{:S(2)}) copy-start(s32[3,256]{1,0:T(4,128)} %grid_ref.1) | copy-start | bytes 9220
  3.1 0.7 %copy-start.3 = (s32[16]{0:T(128)S(1)}, s32[16]{0:T(128)}, u32[]{:S(2)}) copy-start(s32[16]{0:T(128)} %bins_ref.1) | copy-start | bytes 196

commit v2 on v1

v2 whole, which is shorter than its diff:
```python
import jax
import jax.numpy as jnp
from jax import lax
from jax.experimental import pallas as pl
from jax.experimental.pallas import tpu as pltpu
from jax.sharding import PartitionSpec as P

MESH = pl.DeviceIdType.MESH

SIN_COEF = (4.442883014678955, -7.308245658874512, 3.606354236602783, -0.8461116552352905, 0.1098245158791542)
COS_COEF = (1.4142135381698608, -6.978850841522217, 5.739460468292236, -1.883557915687561, 0.3106880187988281)

XS, ZS, BINS = 4, 16, 16
CH_LOC, SNAP_LOC, SAMP, BLOCK = 32, 32, 256, 256
CH = 1024
NEAR = (0, 1, 15, 2, 14, 3, 13, 4, 12, 5, 11, 6, 10, 7, 9, 8)
STEPS = (0, 3, 1, 2)


def horner(coef, z):
    acc = coef[-1] * z + coef[-2]
    for value in coef[-3::-1]:
        acc = acc * z + value
    return acc


def sincos_turns(turns):
    r = turns - jnp.round(turns)
    z = r * r
    s = horner(SIN_COEF, z) * r
    c = horner(COS_COEF, z)
    return 1.0 - s * s, s * c


def lattice(coords, flip):
    c = coords.astype(jnp.float32)
    norm = jnp.sum(c * c, axis=0, keepdims=True)
    high = jnp.floor(norm * (1.0 / 128.0)) * 128.0
    low = norm - high
    one = jnp.ones_like(norm)
    tail = (high, low, one, one) if flip else (one, one, high, low)
    scale = 1.0 if flip else -2.0
    zeros = jnp.zeros((9, c.shape[1]), jnp.float32)
    return jnp.concatenate([c * scale, *tail, zeros], axis=0)


def kernel(
    bins_hbm, sensor_hbm, grid_hbm, series_hbm, bin_power_ref, power_ref,
    bins_ref, sensor_ref, grid_ref, series_v, table_v, sensors_t, sensors_z, points_own, points, spec_f32,
    send1, recv1, slots, turned, wave_c, wave_s, sums, part, recv_a, out_b, recv_b,
    bins_sem, sensor_sem, grid_sem, series_sem, points_send, points_recv, send1_sem, recv1_sem, send2_sem, recv2_sem,
    send_a, sem_a, send_b, sem_b,
):
    f = lax.axis_index("freq")
    g = lax.axis_index("grid")
    core, x, y_hi = lax.rem(f, 2), lax.rem(f // 2, XS), f // (2 * XS)
    x_hi, x_lo = x // 2, lax.rem(x, 2)
    z, y_lo = lax.rem(g, ZS), g // ZS
    pos = x_lo * 2 + core
    own8 = pos * 2 + y_lo
    share = x_hi * 2 + y_hi
    ahead = lax.rem(pos + ZS - z, 4)
    home = ahead == 0

    def group_member(k):
        other = lax.rem(own8 + k, 8)
        lo, place = lax.rem(other, 2), other // 2
        xo = x_hi * 2 + place // 2
        return lo, place, ((y_hi * XS + xo) * 2 + lax.rem(place, 2), lo * ZS + z)

    def z_partner(k):
        zo = lax.rem(z + k, ZS)
        return zo, (f, y_lo * ZS + zo)

    loads = [
        pltpu.make_async_copy(*pair)
        for pair in (
            (bins_hbm, bins_ref, bins_sem),
            (series_hbm, series_v, series_sem),
            (grid_hbm, grid_ref, grid_sem),
            (sensor_hbm, sensor_ref, sensor_sem),
        )
    ]
    for load in loads:
        load.start()

    barrier = pltpu.get_barrier_semaphore()
    for k in NEAR[:0:-1]:
        pl.semaphore_signal(barrier, inc=1, device_id=z_partner(k)[1], device_id_type=MESH)
    for k in range(1, 4):
        other = lax.rem(share + k, 4)
        for place in range(4):
            fo = (lax.rem(other, 2) * XS + (other // 2) * 2 + place // 2) * 2 + place % 2
            pl.semaphore_signal(barrier, inc=1, device_id=(fo, g), device_id_type=MESH)
    for k in range(1, 8):
        pl.semaphore_signal(barrier, inc=1, device_id=group_member(k)[2], device_id_type=MESH)

    loads[0].wait()
    row = lax.broadcasted_iota(jnp.int32, (2 * BINS, SAMP), 0)
    time = lax.broadcasted_iota(jnp.int32, (2 * BINS, SAMP), 1)
    number = jnp.zeros((2 * BINS, SAMP), jnp.int32)
    for b in range(BINS):
        number = jnp.where(row // 2 == b, bins_ref[b], number)
    cycles = (number * time + (row % 2) * (SAMP // 4)) & (SAMP - 1)
    table_v[...] = (sincos_turns(cycles.astype(jnp.float32) * (1.0 / SAMP))[0] * (SAMP / 2.0) ** -0.5).astype(
        jnp.bfloat16
    )

    loads[1].wait()
    spec = lax.dot_general(
        table_v[...], series_v[...].reshape(SNAP_LOC * CH_LOC, SAMP),
        (((1,), (1,)), ((), ())), preferred_element_type=jnp.float32,
    )
    for t in range(8):
        spec_f32[:, t, :] = spec[:, t * 128:(t + 1) * 128]
    send1[...] = spec_f32[...].reshape(BINS, 16, 128).astype(jnp.bfloat16)

    loads[2].wait()
    points_own[...] = lattice(grid_ref[...], False).astype(jnp.bfloat16)

    loads[3].wait()
    sensors_t[...] = jnp.transpose(
        jnp.concatenate([lattice(sensor_ref[...], True), jnp.zeros((112, CH), jnp.float32)], axis=0)
    ).astype(jnp.bfloat16)
    for p in range(ZS):
        for lo in range(2):
            start = pl.multiple_of((lo * ZS + lax.rem(z + NEAR[p], ZS)) * CH_LOC, CH_LOC)
            to = (2 * (p // 4) + lo) * 128 + (p % 4) * CH_LOC
            sensors_z[to:to + CH_LOC, :] = sensors_t[pl.ds(start, CH_LOC), :]
    rate = bins_ref[z].astype(jnp.float32) * (1.0 / 128.0)

    pl.semaphore_wait(barrier, ZS - 1 + 12 + 7)

    @pl.when(home)
    def _():
        for k in NEAR[:0:-1]:
            slot = STEPS.index((ZS - k) // 4)
            pltpu.make_async_remote_copy(
                points_own, points.at[slot], points_send, points_recv.at[slot],
                device_id=z_partner(k)[1], device_id_type=MESH,
            ).start()
        pltpu.make_async_copy(points_own, points.at[0], points_recv.at[0]).start()

    for k in NEAR[:0:-1]:
        zo, device = z_partner(k)
        place = NEAR.index(ZS - k)
        pltpu.make_async_remote_copy(
            send1.at[zo], recv1.at[place], send1_sem, recv1_sem.at[place // 4], device_id=device, device_id_type=MESH
        ).start()
    pltpu.make_async_copy(send1.at[z], recv1.at[0], recv1_sem.at[0]).start()

    def replicas(i):
        pltpu.make_async_copy(points.at[i], points.at[i], points_recv.at[i]).wait()
        rhs = points[i]

        def body(n, carry):
            rows = pl.ds(pl.multiple_of(n * 128, 128), 128)
            squared = jnp.dot(sensors_z[rows, :16], rhs, preferred_element_type=jnp.float32)
            root = lax.rsqrt(jnp.maximum(squared, 0.5))
            c, s = sincos_turns((squared * rate) * root)
            wave_c[i, rows, :] = c.astype(jnp.bfloat16)
            wave_s[i, rows, :] = s.astype(jnp.bfloat16)
            return carry

        lax.fori_loop(0, CH // 128, body, 0)

    lane = lax.broadcasted_iota(jnp.int32, (16, 128), 1) // 32

    def regroup(q):
        four = recv1.at[4 * q:4 * q + 4]
        pltpu.make_async_copy(four, four, recv1_sem.at[q]).wait()
        pieces = [recv1[4 * q + j].astype(jnp.float32) for j in range(4)]
        tiles = []
        for h in range(4):
            tile = None
            for j in range(4):
                shift = ((j - h) * 32) % 128
                moved = pieces[j] if shift == 0 else pltpu.roll(pieces[j], shift, 1)
                tile = moved if tile is None else jnp.where(lane == j, moved, tile)
            tiles.append(tile)
        stacked = jnp.concatenate([t[:8] for t in tiles] + [t[8:] for t in tiles], axis=0)
        mine = pl.ds(pl.multiple_of(pos * 64, 64), 64)
        slots[q, y_lo, mine, :] = stacked.astype(jnp.bfloat16)
        block = slots.at[q, y_lo, mine]
        for k in range(1, 8):
            pltpu.make_async_remote_copy(
                block, block, send2_sem, recv2_sem.at[q, own8],
                device_id=group_member(k)[2], device_id_type=MESH,
            ).start()

    def collect(q):
        for k in range(1, 8):
            lo, place, _ = group_member(k)
            block = slots.at[q, lo, pl.ds(pl.multiple_of(place * 64, 64), 64)]
            pltpu.make_async_copy(block, block, recv2_sem.at[q, lax.rem(own8 + k, 8)]).wait()
        for lo in range(2):
            for p in range(4):
                turned[q, lo, p * 64:p * 64 + 32] = -slots[q, lo, p * 64 + 32:p * 64 + 64]
                turned[q, lo, p * 64 + 32:p * 64 + 64] = slots[q, lo, p * 64:p * 64 + 32]

    def product(i, q):
        rows = slice(q * 256, q * 256 + 256)
        direct = jnp.concatenate([slots[q, 0], slots[q, 1]], axis=1)
        crossed = jnp.concatenate([turned[q, 0], turned[q, 1]], axis=1)
        return jnp.dot(direct, wave_c[i, rows, :], preferred_element_type=jnp.float32) + jnp.dot(
            crossed, wave_s[i, rows, :], preferred_element_type=jnp.float32
        )

    replicas(0)
    regroup(0)
    regroup(1)
    replicas(1)
    regroup(2)
    replicas(2)
    regroup(3)
    replicas(3)
    for q in range(3):
        collect(q)
    for i in range(4):
        sums[i] = (product(i, 0) + product(i, 1)) + product(i, 2)
    collect(3)

    for i in range(4):
        beam = sums[i] + product(i, 3)
        part[i] = jnp.sum(beam * beam, axis=0, keepdims=True) * (1.0 / (512.0 * 1024.0))

        def send():
            target = z_partner(ahead + 4 * STEPS[i])[1]
            pltpu.make_async_remote_copy(
                part.at[i], recv_a.at[z], send_a, sem_a, device_id=target, device_id_type=MESH
            ).start()

        if i > 0:
            send()
        else:
            pl.when(jnp.logical_not(home))(send)

            @pl.when(home)
            def _():
                pltpu.make_async_copy(part.at[0], recv_a.at[z], sem_a).start()

    @pl.when(home)
    def _():
        pltpu.make_async_copy(recv_a, recv_a, sem_a).wait()
        total = recv_a[0]
        for b in range(1, BINS):
            total = total + recv_a[b]
        for b in range(BINS):
            out_b[b, :, :BLOCK] = recv_a[b]
            out_b[b, :, BLOCK:] = total
        for k in range(1, BINS):
            fo = lax.rem(f + k, BINS)
            pltpu.make_async_remote_copy(
                out_b.at[fo], recv_b.at[share], send_b, sem_b, device_id=(fo, g), device_id_type=MESH
            ).start()
        pltpu.make_async_copy(out_b.at[f], recv_b.at[share], sem_b).start()

    pltpu.make_async_copy(recv_b, recv_b, sem_b).wait()
    both = (recv_b[0] + recv_b[1]) + (recv_b[2] + recv_b[3])
    bin_power_ref[...] = both[:, :BLOCK]
    power_ref[...] = both[:, BLOCK:] * (1.0 / BINS)

    @pl.when(home)
    def _():
        sent = wave_c.at[0, 0:15 * 16]
        pltpu.make_async_copy(sent, sent, points_send).wait()
        pltpu.make_async_copy(out_b.at[0:15], out_b.at[0:15], send_b).wait()
        pltpu.make_async_copy(part.at[0:3], part.at[0:3], send_a).wait()

    @pl.when(jnp.logical_not(home))
    def _():
        pltpu.make_async_copy(part, part, send_a).wait()

    pltpu.make_async_copy(send1.at[0:15], send1.at[0:15], send1_sem).wait()
    sent = wave_c.at[:, 0:7 * 32]
    pltpu.make_async_copy(sent, sent, send2_sem).wait()


def on_device(series, bins, sensor_coords, grid_coords):
    vmem = pltpu.VMEM
    bf16, f32 = jnp.bfloat16, jnp.float32
    dma = pltpu.SemaphoreType.DMA
    bin_power, power = pl.pallas_call(
        kernel,
        out_shape=(jax.ShapeDtypeStruct((1, BLOCK), f32), jax.ShapeDtypeStruct((1, BLOCK), f32)),
        in_specs=[pl.BlockSpec(memory_space=pltpu.HBM)] * 4,
        out_specs=(pl.BlockSpec(memory_space=vmem), pl.BlockSpec(memory_space=vmem)),
        scratch_shapes=[
            pltpu.SMEM((BINS,), jnp.int32),
            vmem((3, CH), jnp.int32),
            vmem((3, BLOCK), jnp.int32),
            vmem((SNAP_LOC, CH_LOC, SAMP), bf16),
            vmem((2 * BINS, SAMP), bf16),
            vmem((CH, 128), bf16),
            vmem((CH, 128), bf16),
            vmem((16, BLOCK), bf16),
            vmem((4, 16, BLOCK), bf16),
            vmem((2 * BINS, 8, 128), f32),
            vmem((BINS, 16, 128), bf16),
            vmem((ZS, 16, 128), bf16),
            vmem((4, 2, 256, 128), bf16),
            vmem((4, 2, 256, 128), bf16),
            vmem((4, CH, BLOCK), bf16),
            vmem((4, CH, BLOCK), bf16),
            vmem((4, 256, BLOCK), f32),
            vmem((4, 1, BLOCK), f32),
            vmem((BINS, 1, BLOCK), f32),
            vmem((BINS, 1, 2 * BLOCK), f32),
            vmem((4, 1, 2 * BLOCK), f32),
            dma, dma, dma, dma, dma, dma((4,)), dma, dma((4,)), dma, dma((4, 8)), dma, dma, dma, dma,
        ],
        compiler_params=pltpu.CompilerParams(
            collective_id=0, has_side_effects=True, vmem_limit_bytes=56 * 1024 * 1024
        ),
    )(bins, sensor_coords, grid_coords, series)
    return bin_power, power.reshape(BLOCK)


def solution(mesh):
    return jax.shard_map(
        on_device,
        mesh=mesh,
        in_specs=(P("freq", "grid", None), P(), P(), P(None, "grid")),
        out_specs=(P("freq", "grid"), P("grid")),
        check_vma=False,
    )
```

time: 52.2 us -> 48.1 us (0.921)
  local copies, waits for them, and re-layouts: 4.22 us -> 1.86 us
  Pallas kernels: 47.1 us -> 45.4 us
    unnamed x10 -> x6, local copies, waits for them, and re-layouts: 4.22 us -> 1.86 us
    pallas_call x1, Pallas kernels: 47.1 us -> 45.4 us  [on_device(): pl.pallas_call(kernel, out_shape=(jax.ShapeDtypeStruct((1, BLOCK), f32),...]
where the time goes in v2:
time: 48.1 us; the launch traced here: 47.9 us
  Pallas kernels  45.4 us (94%)
  local copies, waits for them, and re-layouts  1.86 us (4%)
  between operations  0.65 us (1%)
    pallas_call x1, Pallas kernels, on_device(): pl.pallas_call(kernel, out_shape=(jax.ShapeDtypeStruct((1, BLOCK), f32),...  45.4 us
    unnamed x6, local copies, waits for them, and re-layouts  1.86 us

profile of v2, /device:TPU:1, one launch (start us, length us, event | category | flops | bytes accessed | tf_op | source)
XLA Modules:
  0.0 47.9 jit_solution(13397440031954973624)
XLA Ops:
  0.6 45.4 %shard_map.59 = (f32[1,256]{1,0:T(1,128)}, f32[1,256]{1,0:T(1,128)}) custom-call(s32[16]{0:T(128)} %bins_hbm.1, s32[3,1024]{1,0:T(4,128)} %sensor_hbm.1, s32[3,256]{1,0:T(4,128)} %grid_hbm.1, bf16[32,32,256]{2,1,0:T(8,128)(2,1)} %series_hbm.1), custom_call_target="tpu_custom_call" | custom-call | tf_op jit(solution)/shard_map/pallas_call | solution.py:283
  46.0 0.0 copy-start.1
  46.0 0.7 %copy-done.1 = f32[1,256]{1,0:T(1,128)S(1)} copy-done((f32[1,256]{1,0:T(1,128)S(1)}, f32[1,256]{1,0:T(1,128)}, u32[]{:S(2)}) %copy-start.1) | copy-done | bytes 1048
  46.7 0.0 copy-start
  46.7 0.6 %copy.8 = f32[1,256]{1,0:T(1,128)} copy(f32[1,256]{1,0:T(1,128)S(1)} %copy-done.1) | data formatting | bytes 2048
  47.3 0.1 copy-done
  47.3 0.6 %copy.9 = f32[256]{0:T(256)} copy(f32[256]{0:T(256)S(1)} %bitcast.1) | data formatting | bytes 2048
Async XLA Ops:
  46.0 0.7 %copy-start.1 = (f32[1,256]{1,0:T(1,128)S(1)}, f32[1,256]{1,0:T(1,128)}, u32[]{:S(2)}) copy-start(f32[1,256]{1,0:T(1,128)} %get-tuple-element.8) | copy-start | bytes 3076
  46.7 0.6 %copy-start = (f32[1,256]{1,0:T(1,128)S(1)}, f32[1,256]{1,0:T(1,128)}, u32[]{:S(2)}) copy-start(f32[1,256]{1,0:T(1,128)} %get-tuple-element.5) | copy-start | bytes 3076

commit v3 on v2

--- a/solution.py
+++ b/solution.py
@@ -46,7 +46,7 @@
 
 def kernel(
     bins_hbm, sensor_hbm, grid_hbm, series_hbm, bin_power_ref, power_ref,
-    bins_ref, sensor_ref, grid_ref, series_v, table_v, sensors_t, sensors_z, points_own, points, spec_f32,
+    bins_ref, sensor_ref, grid_ref, series_v, table_v, sensors_t, sensors_z, points, spec_f32,
     send1, recv1, slots, turned, wave_c, wave_s, sums, part, recv_a, out_b, recv_b,
     bins_sem, sensor_sem, grid_sem, series_sem, points_send, points_recv, send1_sem, recv1_sem, send2_sem, recv2_sem,
     send_a, sem_a, send_b, sem_b,
@@ -59,7 +59,7 @@
     pos = x_lo * 2 + core
     own8 = pos * 2 + y_lo
     share = x_hi * 2 + y_hi
-    ahead = lax.rem(pos + ZS - z, 4)
+    ahead = lax.rem((1 - core) * 2 + x_lo + ZS - z, 4)
     home = ahead == 0
 
     def group_member(k):
@@ -115,9 +115,6 @@
         spec_f32[:, t, :] = spec[:, t * 128:(t + 1) * 128]
     send1[...] = spec_f32[...].reshape(BINS, 16, 128).astype(jnp.bfloat16)
 
-    loads[2].wait()
-    points_own[...] = lattice(grid_ref[...], False).astype(jnp.bfloat16)
-
     loads[3].wait()
     sensors_t[...] = jnp.transpose(
         jnp.concatenate([lattice(sensor_ref[...], True), jnp.zeros((112, CH), jnp.float32)], axis=0)
@@ -131,16 +128,6 @@
 
     pl.semaphore_wait(barrier, ZS - 1 + 12 + 7)
 
-    @pl.when(home)
-    def _():
-        for k in NEAR[:0:-1]:
-            slot = STEPS.index((ZS - k) // 4)
-            pltpu.make_async_remote_copy(
-                points_own, points.at[slot], points_send, points_recv.at[slot],
-                device_id=z_partner(k)[1], device_id_type=MESH,
-            ).start()
-        pltpu.make_async_copy(points_own, points.at[0], points_recv.at[0]).start()
-
     for k in NEAR[:0:-1]:
         zo, device = z_partner(k)
         place = NEAR.index(ZS - k)
@@ -149,9 +136,24 @@
         ).start()
     pltpu.make_async_copy(send1.at[z], recv1.at[0], recv1_sem.at[0]).start()
 
+    @pl.when(home)
+    def _():
+        loads[2].wait()
+        for k in NEAR[:0:-1]:
+            slot = STEPS.index((ZS - k) // 4)
+            pltpu.make_async_remote_copy(
+                grid_ref, points.at[slot], points_send, points_recv.at[slot],
+                device_id=z_partner(k)[1], device_id_type=MESH,
+            ).start()
+        pltpu.make_async_copy(grid_ref, points.at[0], points_recv.at[0]).start()
+
+    @pl.when(jnp.logical_not(home))
+    def _():
+        loads[2].wait()
+
     def replicas(i):
         pltpu.make_async_copy(points.at[i], points.at[i], points_recv.at[i]).wait()
-        rhs = points[i]
+        rhs = lattice(points[i], False).astype(jnp.bfloat16)
 
         def body(n, carry):
             rows = pl.ds(pl.multiple_of(n * 128, 128), 128)
@@ -262,8 +264,9 @@
 
     @pl.when(home)
     def _():
-        sent = wave_c.at[0, 0:15 * 16]
-        pltpu.make_async_copy(sent, sent, points_send).wait()
+        for _ in range(3):
+            pltpu.make_async_copy(points, points, points_send).wait()
+        pltpu.make_async_copy(points.at[0:3], points.at[0:3], points_send).wait()
         pltpu.make_async_copy(out_b.at[0:15], out_b.at[0:15], send_b).wait()
         pltpu.make_async_copy(part.at[0:3], part.at[0:3], send_a).wait()
 
@@ -293,8 +296,7 @@
             vmem((2 * BINS, SAMP), bf16),
             vmem((CH, 128), bf16),
             vmem((CH, 128), bf16),
-            vmem((16, BLOCK), bf16),
-            vmem((4, 16, BLOCK), bf16),
+            vmem((4, 3, BLOCK), jnp.int32),
             vmem((2 * BINS, 8, 128), f32),
             vmem((BINS, 16, 128), bf16),
             vmem((ZS, 16, 128), bf16),

time: 48.1 us -> 46.6 us (0.969)
  Pallas kernels: 45.4 us -> 43.9 us
    pallas_call x1, Pallas kernels: 45.4 us -> 43.9 us  [on_device(): pl.pallas_call(kernel, out_shape=(jax.ShapeDtypeStruct((1, BLOCK), f32),...]
where the time goes in v3:
time: 46.6 us; the launch traced here: 46.4 us
  Pallas kernels  43.9 us (94%)
  local copies, waits for them, and re-layouts  1.86 us (4%)
  between operations  0.65 us (1%)
    pallas_call x1, Pallas kernels, on_device(): pl.pallas_call(kernel, out_shape=(jax.ShapeDtypeStruct((1, BLOCK), f32),...  43.9 us
    unnamed x6, local copies, waits for them, and re-layouts  1.86 us

profile of v3, /device:TPU:1, one launch (start us, length us, event | category | flops | bytes accessed | tf_op | source)
XLA Modules:
  0.0 46.4 jit_solution(2842016481539279559)
XLA Ops:
  0.6 43.9 %shard_map.59 = (f32[1,256]{1,0:T(1,128)}, f32[1,256]{1,0:T(1,128)}) custom-call(s32[16]{0:T(128)} %bins_hbm.1, s32[3,1024]{1,0:T(4,128)} %sensor_hbm.1, s32[3,256]{1,0:T(4,128)} %grid_hbm.1, bf16[32,32,256]{2,1,0:T(8,128)(2,1)} %series_hbm.1), custom_call_target="tpu_custom_call" | custom-call | tf_op jit(solution)/shard_map/pallas_call | solution.py:286
  44.6 0.0 copy-start.1
  44.6 0.7 %copy-done.1 = f32[1,256]{1,0:T(1,128)S(1)} copy-done((f32[1,256]{1,0:T(1,128)S(1)}, f32[1,256]{1,0:T(1,128)}, u32[]{:S(2)}) %copy-start.1) | copy-done | bytes 1048
  45.2 0.0 copy-start
  45.2 0.6 %copy.8 = f32[1,256]{1,0:T(1,128)} copy(f32[1,256]{1,0:T(1,128)S(1)} %copy-done.1) | data formatting | bytes 2048
  45.8 0.1 copy-done
  45.9 0.6 %copy.9 = f32[256]{0:T(256)} copy(f32[256]{0:T(256)S(1)} %bitcast.1) | data formatting | bytes 2048
Async XLA Ops:
  44.6 0.7 %copy-start.1 = (f32[1,256]{1,0:T(1,128)S(1)}, f32[1,256]{1,0:T(1,128)}, u32[]{:S(2)}) copy-start(f32[1,256]{1,0:T(1,128)} %get-tuple-element.8) | copy-start | bytes 3076
  45.2 0.6 %copy-start = (f32[1,256]{1,0:T(1,128)S(1)}, f32[1,256]{1,0:T(1,128)}, u32[]{:S(2)}) copy-start(f32[1,256]{1,0:T(1,128)} %get-tuple-element.5) | copy-start | bytes 3076

commit v4 on v3

--- a/solution.py
+++ b/solution.py
@@ -45,7 +45,7 @@
 
 
 def kernel(
-    bins_hbm, sensor_hbm, grid_hbm, series_hbm, bin_power_ref, power_ref,
+    bins_hbm, sensor_hbm, grid_hbm, series_hbm, out_ref,
     bins_ref, sensor_ref, grid_ref, series_v, table_v, sensors_t, sensors_z, points, spec_f32,
     send1, recv1, slots, turned, wave_c, wave_s, sums, part, recv_a, out_b, recv_b,
     bins_sem, sensor_sem, grid_sem, series_sem, points_send, points_recv, send1_sem, recv1_sem, send2_sem, recv2_sem,
@@ -216,10 +216,13 @@
     replicas(2)
     regroup(3)
     replicas(3)
-    for q in range(3):
-        collect(q)
+    collect(0)
+    collect(1)
     for i in range(4):
-        sums[i] = (product(i, 0) + product(i, 1)) + product(i, 2)
+        sums[i] = product(i, 0) + product(i, 1)
+    collect(2)
+    for i in range(4):
+        sums[i] += product(i, 2)
     collect(3)
 
     for i in range(4):
@@ -259,8 +262,7 @@
 
     pltpu.make_async_copy(recv_b, recv_b, sem_b).wait()
     both = (recv_b[0] + recv_b[1]) + (recv_b[2] + recv_b[3])
-    bin_power_ref[...] = both[:, :BLOCK]
-    power_ref[...] = both[:, BLOCK:] * (1.0 / BINS)
+    out_ref[...] = both
 
     @pl.when(home)
     def _():
@@ -283,11 +285,11 @@
     vmem = pltpu.VMEM
     bf16, f32 = jnp.bfloat16, jnp.float32
     dma = pltpu.SemaphoreType.DMA
-    bin_power, power = pl.pallas_call(
+    both = pl.pallas_call(
         kernel,
-        out_shape=(jax.ShapeDtypeStruct((1, BLOCK), f32), jax.ShapeDtypeStruct((1, BLOCK), f32)),
+        out_shape=vmem((1, 2 * BLOCK), f32),
         in_specs=[pl.BlockSpec(memory_space=pltpu.HBM)] * 4,
-        out_specs=(pl.BlockSpec(memory_space=vmem), pl.BlockSpec(memory_space=vmem)),
+        out_specs=pl.BlockSpec(memory_space=vmem),
         scratch_shapes=[
             pltpu.SMEM((BINS,), jnp.int32),
             vmem((3, CH), jnp.int32),
@@ -315,7 +317,7 @@
             collective_id=0, has_side_effects=True, vmem_limit_bytes=56 * 1024 * 1024
         ),
     )(bins, sensor_coords, grid_coords, series)
-    return bin_power, power.reshape(BLOCK)
+    return both[:, :BLOCK], both[0, BLOCK:] * (1.0 / BINS)
 
 
 def solution(mesh):

time: 46.6 us -> 44.7 us (0.959)
  local copies, waits for them, and re-layouts: 1.86 us -> 0 us
  other arithmetic: 0 us -> 0.57 us
  Pallas kernels: 43.9 us -> 43.4 us
    unnamed x6 -> x0, local copies, waits for them, and re-layouts: 1.86 us -> none
    pallas_call x1, Pallas kernels: 43.9 us -> 43.4 us  [on_device(): pl.pallas_call(kernel, out_shape=vmem((1, 2 * BLOCK), f32), in_specs=[pl....]
    mul x0 -> x1, other arithmetic: none -> 0.57 us  [on_device(): return (both[:, :BLOCK], both[0, BLOCK:] * (1.0 / BINS))]
where the time goes in v4:
time: 44.7 us; the launch traced here: 44.6 us
  Pallas kernels  43.4 us (97%)
  between operations  0.64 us (1%)
  other arithmetic  0.57 us (1%)
    pallas_call x1, Pallas kernels, on_device(): pl.pallas_call(kernel, out_shape=vmem((1, 2 * BLOCK), f32), in_specs=[pl....  43.4 us

profile of v4, /device:TPU:1, one launch (start us, length us, event | category | flops | bytes accessed | tf_op | source)
XLA Modules:
  0.0 44.6 jit_solution(10510722819413590912)
XLA Ops:
  0.6 43.4 %shard_map.59 = f32[1,512]{1,0:T(1,128)S(1)} custom-call(s32[16]{0:T(128)} %bins_hbm.1, s32[3,1024]{1,0:T(4,128)} %sensor_hbm.1, s32[3,256]{1,0:T(4,128)} %grid_hbm.1, bf16[32,32,256]{2,1,0:T(8,128)(2,1)} %series_hbm.1), custom_call_target="tpu_custom_call" | custom-call | tf_op jit(solution)/shard_map/pallas_call | solution.py:288
  44.0 0.6 %slice_multiply_fusion = (f32[1,256]{1,0:T(1,128)}, f32[1,256]{1,0:T(1,128)}) fusion(f32[1,512]{1,0:T(1,128)S(1)} %shard_map.59), kind=kLoop, calls=%fused_computation | loop fusion | flops 256 | bytes 4096 | tf_op jit(solution)/shard_map/mul | solution.py:320

commit v5 on v4

--- a/solution.py
+++ b/solution.py
@@ -59,8 +59,9 @@
     pos = x_lo * 2 + core
     own8 = pos * 2 + y_lo
     share = x_hi * 2 + y_hi
-    ahead = lax.rem((1 - core) * 2 + x_lo + ZS - z, 4)
-    home = ahead == 0
+    ahead = lax.rem((1 - core) * 2 + 1 - x_lo + ZS - z, 4)
+    holds = ahead == 0
+    home = jnp.logical_and(core == 1, lax.rem(z, 2) != x_lo)
 
     def group_member(k):
         other = lax.rem(own8 + k, 8)
@@ -128,7 +129,7 @@
 
     pl.semaphore_wait(barrier, ZS - 1 + 12 + 7)
 
-    for k in NEAR[:0:-1]:
+    for k in NEAR[1:]:
         zo, device = z_partner(k)
         place = NEAR.index(ZS - k)
         pltpu.make_async_remote_copy(
@@ -136,7 +137,7 @@
         ).start()
     pltpu.make_async_copy(send1.at[z], recv1.at[0], recv1_sem.at[0]).start()
 
-    @pl.when(home)
+    @pl.when(holds)
     def _():
         loads[2].wait()
         for k in NEAR[:0:-1]:
@@ -147,7 +148,7 @@
             ).start()
         pltpu.make_async_copy(grid_ref, points.at[0], points_recv.at[0]).start()
 
-    @pl.when(jnp.logical_not(home))
+    @pl.when(jnp.logical_not(holds))
     def _():
         loads[2].wait()
 
@@ -208,13 +209,13 @@
             crossed, wave_s[i, rows, :], preferred_element_type=jnp.float32
         )
 
+    regroup(0)
     replicas(0)
-    regroup(0)
     regroup(1)
     replicas(1)
     regroup(2)
+    regroup(3)
     replicas(2)
-    regroup(3)
     replicas(3)
     collect(0)
     collect(1)
@@ -230,7 +231,7 @@
         part[i] = jnp.sum(beam * beam, axis=0, keepdims=True) * (1.0 / (512.0 * 1024.0))
 
         def send():
-            target = z_partner(ahead + 4 * STEPS[i])[1]
+            target = (f + 1 - core, z_partner(ahead + 4 * STEPS[i])[1][1])
             pltpu.make_async_remote_copy(
                 part.at[i], recv_a.at[z], send_a, sem_a, device_id=target, device_id_type=MESH
             ).start()
@@ -238,9 +239,10 @@
         if i > 0:
             send()
         else:
-            pl.when(jnp.logical_not(home))(send)
-
-            @pl.when(home)
+            stays = jnp.logical_and(holds, core == 1)
+            pl.when(jnp.logical_not(stays))(send)
+
+            @pl.when(stays)
             def _():
                 pltpu.make_async_copy(part.at[0], recv_a.at[z], sem_a).start()
 
@@ -264,17 +266,21 @@
     both = (recv_b[0] + recv_b[1]) + (recv_b[2] + recv_b[3])
     out_ref[...] = both
 
-    @pl.when(home)
+    @pl.when(holds)
     def _():
         for _ in range(3):
             pltpu.make_async_copy(points, points, points_send).wait()
         pltpu.make_async_copy(points.at[0:3], points.at[0:3], points_send).wait()
+
+    @pl.when(home)
+    def _():
         pltpu.make_async_copy(out_b.at[0:15], out_b.at[0:15], send_b).wait()
-        pltpu.make_async_copy(part.at[0:3], part.at[0:3], send_a).wait()
-
-    @pl.when(jnp.logical_not(home))
-    def _():
-        pltpu.make_async_copy(part, part, send_a).wait()
+
+    pltpu.make_async_copy(part.at[0:3], part.at[0:3], send_a).wait()
+
+    @pl.when(jnp.logical_not(jnp.logical_and(holds, core == 1)))
+    def _():
+        pltpu.make_async_copy(part.at[0], part.at[0], send_a).wait()
 
     pltpu.make_async_copy(send1.at[0:15], send1.at[0:15], send1_sem).wait()
     sent = wave_c.at[:, 0:7 * 32]

time: 44.7 us -> 43.5 us (0.973)
  Pallas kernels: 43.4 us -> 42.2 us
    pallas_call x1, Pallas kernels: 43.4 us -> 42.2 us  [on_device(): pl.pallas_call(kernel, out_shape=vmem((1, 2 * BLOCK), f32), in_specs=[pl....]
where the time goes in v5:
time: 43.5 us; the launch traced here: 43.4 us
  Pallas kernels  42.2 us (97%)
  between operations  0.64 us (1%)
  other arithmetic  0.57 us (1%)
    pallas_call x1, Pallas kernels, on_device(): pl.pallas_call(kernel, out_shape=vmem((1, 2 * BLOCK), f32), in_specs=[pl....  42.2 us

profile of v5, /device:TPU:1, one launch (start us, length us, event | category | flops | bytes accessed | tf_op | source)
XLA Modules:
  0.0 43.4 jit_solution(3804844706918934579)
XLA Ops:
  0.6 42.2 %shard_map.59 = f32[1,512]{1,0:T(1,128)S(1)} custom-call(s32[16]{0:T(128)} %bins_hbm.1, s32[3,1024]{1,0:T(4,128)} %sensor_hbm.1, s32[3,256]{1,0:T(4,128)} %grid_hbm.1, bf16[32,32,256]{2,1,0:T(8,128)(2,1)} %series_hbm.1), custom_call_target="tpu_custom_call" | custom-call | tf_op jit(solution)/shard_map/pallas_call | solution.py:294
  42.8 0.6 %slice_multiply_fusion = (f32[1,256]{1,0:T(1,128)}, f32[1,256]{1,0:T(1,128)}) fusion(f32[1,512]{1,0:T(1,128)S(1)} %shard_map.59), kind=kLoop, calls=%fused_computation | loop fusion | flops 256 | bytes 4096 | tf_op jit(solution)/shard_map/mul | solution.py:326

commit v6 on v5

--- a/solution.py
+++ b/solution.py
@@ -140,7 +140,7 @@
     @pl.when(holds)
     def _():
         loads[2].wait()
-        for k in NEAR[:0:-1]:
+        for k in NEAR[1:]:
             slot = STEPS.index((ZS - k) // 4)
             pltpu.make_async_remote_copy(
                 grid_ref, points.at[slot], points_send, points_recv.at[slot],
@@ -226,7 +226,7 @@
         sums[i] += product(i, 2)
     collect(3)
 
-    for i in range(4):
+    for i in (3, 2, 1, 0):
         beam = sums[i] + product(i, 3)
         part[i] = jnp.sum(beam * beam, axis=0, keepdims=True) * (1.0 / (512.0 * 1024.0))
 

time: 43.5 us -> 42.6 us (0.979)
  Pallas kernels: 42.2 us -> 41.2 us
    pallas_call x1, Pallas kernels: 42.2 us -> 41.2 us  [on_device(): pl.pallas_call(kernel, out_shape=vmem((1, 2 * BLOCK), f32), in_specs=[pl....]
where the time goes in v6:
time: 42.6 us; the launch traced here: 42.4 us
  Pallas kernels  41.2 us (97%)
  between operations  0.64 us (2%)
  other arithmetic  0.57 us (1%)
    pallas_call x1, Pallas kernels, on_device(): pl.pallas_call(kernel, out_shape=vmem((1, 2 * BLOCK), f32), in_specs=[pl....  41.2 us

profile of v6, /device:TPU:1, one launch (start us, length us, event | category | flops | bytes accessed | tf_op | source)
XLA Modules:
  0.0 42.4 jit_solution(12462042526035679508)
XLA Ops:
  0.6 41.2 %shard_map.59 = f32[1,512]{1,0:T(1,128)S(1)} custom-call(s32[16]{0:T(128)} %bins_hbm.1, s32[3,1024]{1,0:T(4,128)} %sensor_hbm.1, s32[3,256]{1,0:T(4,128)} %grid_hbm.1, bf16[32,32,256]{2,1,0:T(8,128)(2,1)} %series_hbm.1), custom_call_target="tpu_custom_call" | custom-call | tf_op jit(solution)/shard_map/pallas_call | solution.py:294
  41.9 0.6 %slice_multiply_fusion = (f32[1,256]{1,0:T(1,128)}, f32[1,256]{1,0:T(1,128)}) fusion(f32[1,512]{1,0:T(1,128)S(1)} %shard_map.59), kind=kLoop, calls=%fused_computation | loop fusion | flops 256 | bytes 4096 | tf_op jit(solution)/shard_map/mul | solution.py:326

commit v7 on v6

--- a/solution.py
+++ b/solution.py
@@ -255,7 +255,7 @@
         for b in range(BINS):
             out_b[b, :, :BLOCK] = recv_a[b]
             out_b[b, :, BLOCK:] = total
-        for k in range(1, BINS):
+        for k in (14, 10, 6, 2, 12, 4, 8, 13, 11, 5, 3, 9, 7, 15, 1):
             fo = lax.rem(f + k, BINS)
             pltpu.make_async_remote_copy(
                 out_b.at[fo], recv_b.at[share], send_b, sem_b, device_id=(fo, g), device_id_type=MESH

time: 42.6 us -> 42.3 us (level)
  no operation moved by 1% of the time
where the time goes in v7:
time: 42.3 us; the launch traced here: 42.2 us
  Pallas kernels  41 us (97%)
  between operations  0.64 us (2%)
  other arithmetic  0.57 us (1%)
    pallas_call x1, Pallas kernels, on_device(): pl.pallas_call(kernel, out_shape=vmem((1, 2 * BLOCK), f32), in_specs=[pl....  41 us

profile of v7, /device:TPU:1, one launch (start us, length us, event | category | flops | bytes accessed | tf_op | source)
XLA Modules:
  0.0 42.2 jit_solution(17147272144117449281)
XLA Ops:
  0.6 41.0 %shard_map.59 = f32[1,512]{1,0:T(1,128)S(1)} custom-call(s32[16]{0:T(128)} %bins_hbm.1, s32[3,1024]{1,0:T(4,128)} %sensor_hbm.1, s32[3,256]{1,0:T(4,128)} %grid_hbm.1, bf16[32,32,256]{2,1,0:T(8,128)(2,1)} %series_hbm.1), custom_call_target="tpu_custom_call" | custom-call | tf_op jit(solution)/shard_map/pallas_call | solution.py:294
  41.6 0.6 %slice_multiply_fusion = (f32[1,256]{1,0:T(1,128)}, f32[1,256]{1,0:T(1,128)}) fusion(f32[1,512]{1,0:T(1,128)S(1)} %shard_map.59), kind=kLoop, calls=%fused_computation | loop fusion | flops 256 | bytes 4096 | tf_op jit(solution)/shard_map/mul | solution.py:326

commit v8 on v7

--- a/solution.py
+++ b/solution.py
@@ -249,9 +249,10 @@
     @pl.when(home)
     def _():
         pltpu.make_async_copy(recv_a, recv_a, sem_a).wait()
-        total = recv_a[0]
-        for b in range(1, BINS):
-            total = total + recv_a[b]
+        terms = [recv_a[b] for b in range(BINS)]
+        while len(terms) > 1:
+            terms = [left + right for left, right in zip(terms[::2], terms[1::2])]
+        total = terms[0]
         for b in range(BINS):
             out_b[b, :, :BLOCK] = recv_a[b]
             out_b[b, :, BLOCK:] = total

time: 42.3 us -> 42.3 us (level)
  no operation moved by 1% of the time
where the time goes in v8:
time: 42.3 us; the launch traced here: 42.2 us
  Pallas kernels  40.9 us (97%)
  between operations  0.64 us (2%)
  other arithmetic  0.57 us (1%)
    pallas_call x1, Pallas kernels, on_device(): pl.pallas_call(kernel, out_shape=vmem((1, 2 * BLOCK), f32), in_specs=[pl....  40.9 us

profile of v8, /device:TPU:1, one launch (start us, length us, event | category | flops | bytes accessed | tf_op | source)
XLA Modules:
  0.0 42.2 jit_solution(2817546097551549171)
XLA Ops:
  0.6 40.9 %shard_map.59 = f32[1,512]{1,0:T(1,128)S(1)} custom-call(s32[16]{0:T(128)} %bins_hbm.1, s32[3,1024]{1,0:T(4,128)} %sensor_hbm.1, s32[3,256]{1,0:T(4,128)} %grid_hbm.1, bf16[32,32,256]{2,1,0:T(8,128)(2,1)} %series_hbm.1), custom_call_target="tpu_custom_call" | custom-call | tf_op jit(solution)/shard_map/pallas_call | solution.py:295
  41.6 0.6 %slice_multiply_fusion = (f32[1,256]{1,0:T(1,128)}, f32[1,256]{1,0:T(1,128)}) fusion(f32[1,512]{1,0:T(1,128)S(1)} %shard_map.59), kind=kLoop, calls=%fused_computation | loop fusion | flops 256 | bytes 4096 | tf_op jit(solution)/shard_map/mul | solution.py:327
